TPU v7x, 256 devices: a whole 4x4x8 slice. The times are simulated.
256 devices in a mesh: dp: 64 (over z, x, core), seq: 4 (over y).
Axes of the slice: x: 4, y: 4, z: 8, core: 2. Of those that a mesh axis runs over, the one named last changes fastest.
Arguments:
- hidden_in: bfloat16 [65536, 4096], P(('dp', 'seq')), may hold values from -24 to 24
- bc_weight: bfloat16 [4096, 256], P('dp'), may hold values from -0.09375 to 0.09375
- values: bfloat16 [65536, 4096], P(('dp', 'seq')), may hold values from -6 to 6
- teacher: bfloat16 [65536, 4096], P(('dp', 'seq')), may hold values from -6 to 6
- decay_codes: int32 [65536, 64], P(('dp', 'seq')), may hold values from 0 to 15
- resets: int32 [65536], P(('dp', 'seq')), may hold values 0 or 1
- head_decay_rates: float32 [64], replicated, may hold values from 0.25 to 100
- skip_gain: float32 [64], replicated, may hold values from 0.5 to 1.5
- confidence: int32 [65536], P(('dp', 'seq')), may hold values from 1 to 8
Outputs:
- values_grad: bfloat16 [65536, 4096], P(('dp', 'seq'))
- hidden_grad: bfloat16 [65536, 4096], P(('dp', 'seq'))
- weight_grad: float32 [4096, 256], P('dp')
All inputs are finite; a program needn't handle non-finite values. No bound on the sum of `resets` on one device may be relied on, other than what follows from the above.
Results may differ from a plain program's by a relative error of at most 0.011.
Values may be sent and summed in bfloat16 or wider, within the bound.
No kernel may reach another device: no remote copies, remote signals or barrier semaphores. Data moves between devices by JAX's collectives and lax.ppermute only.
A program may use at most 128 MiB of HBM per device.

v0:
```python
import math
import jax
import jax.numpy as jnp
from jax import lax
from jax.sharding import PartitionSpec as P

GROUP = 256
SPIKE_MULTIPLIER = 3000.0
STEP_FACTOR = 16.0


def carried_in(x, axis, combine, identity):
    peers, place = (lax.axis_size(axis), lax.axis_index(axis))
    everything = jax.tree.map(lambda part: lax.all_gather(part, axis), x)
    start = jax.tree.map(
        lambda part, zero: jnp.broadcast_to(jnp.asarray(zero, part.dtype), part.shape), x, identity
    )

    def carried_step(k, before):
        reached = k < place
        new = combine(before, jax.tree.map(lambda part: part[k], everything))
        return jax.tree.map(lambda a, b: jnp.where(reached, a, b), new, before)

    return lax.fori_loop(0, peers, carried_step, start)


def prefix(x, axis, combine, identity):
    peers, place = (lax.axis_size(axis), lax.axis_index(axis))
    everything = jax.tree.map(
        lambda part, kind: lax.all_gather(part.astype(kind), axis), x, (jnp.bfloat16, jnp.bfloat16)
    )
    start = jax.tree.map(
        lambda part, zero: jnp.broadcast_to(jnp.asarray(zero, part.dtype), part.shape), x, identity
    )

    def prefix_step(k, before):
        at = peers - 1 - k
        reached = at > place
        new = combine(
            before, jax.tree.map(lambda part, own: part[at].astype(own.dtype), everything, x)
        )
        return jax.tree.map(lambda a, b: jnp.where(reached, a, b), new, before)

    return lax.fori_loop(0, peers, prefix_step, start)


def decay_terms(decay_codes, resets, head_decay_rates):
    logarithm_floor = jnp.log(0.9995 + 0.0004 * decay_codes.astype(jnp.float32) / 15.0)
    decay_logarithm = (
        head_decay_rates[None, :]
        * (1.0 + SPIKE_MULTIPLIER * resets.astype(jnp.float32))[:, None]
        * logarithm_floor
    )
    return (decay_logarithm, -STEP_FACTOR * logarithm_floor)


def combine(earlier, later):
    return (earlier[0] + later[0], jnp.exp(later[0])[:, None, None] * earlier[1] + later[1])


def body(
    hidden_in,
    bc_weight,
    values,
    teacher,
    decay_codes,
    resets,
    head_decay_rates,
    skip_gain,
    confidence,
):
    length = hidden_in.shape[0]
    blocks = length // GROUP
    head_count = decay_codes.shape[1]
    head_size = values.shape[1] // head_count
    state_size = bc_weight.shape[1] // 2
    seq_count = lax.axis_size("seq")
    doc_len = length * seq_count
    all_tokens = doc_len * lax.axis_size("dp")
    conf_float = confidence.astype(jnp.float32)
    conf_total = lax.psum(jnp.sum(conf_float), "seq")
    full_weight = lax.all_gather(bc_weight, "dp", axis=0, tiled=True)
    bc_acc = jnp.dot(hidden_in, full_weight, preferred_element_type=jnp.float32)
    bc_rows = bc_acc.astype(jnp.bfloat16).reshape(blocks, GROUP, 2 * state_size)
    input_map = bc_rows[:, :, :state_size]
    output_map = bc_rows[:, :, state_size:]
    decay_logarithm, step_size = decay_terms(decay_codes, resets, head_decay_rates)
    cumulative = jnp.cumsum(decay_logarithm.reshape(blocks, GROUP, head_count), axis=1)
    step_blk = step_size.reshape(blocks, GROUP, head_count)
    block_log = cumulative[:, -1, :]
    tail_decay = jnp.exp(block_log[:, None, :] - cumulative)
    leading_decay = jnp.exp(cumulative)
    cum_heads = jnp.transpose(cumulative, (0, 2, 1))
    lower_tri = lax.broadcasted_iota(jnp.int32, (GROUP, GROUP), 0) >= lax.broadcasted_iota(
        jnp.int32, (GROUP, GROUP), 1
    )
    spread = jnp.where(lower_tri, cum_heads[:, :, :, None] - cum_heads[:, :, None, :], 0.0)
    decay_grid = (
        jnp.where(lower_tri, jnp.exp(spread), 0.0)
        * jnp.transpose(step_blk, (0, 2, 1))[:, :, None, :]
    )
    intersection = jnp.einsum(
        "btn,bsn->bts", output_map, input_map, preferred_element_type=jnp.float32
    )
    mixing = (intersection[:, None] * decay_grid).astype(jnp.bfloat16)
    value_blocks = values.reshape(blocks, GROUP, head_count, head_size)
    write_scale = tail_decay * step_blk
    value_scaled = (write_scale[..., None] * value_blocks).astype(jnp.bfloat16)
    local_state = jnp.einsum(
        "bshp,bsn->bhpn", value_scaled, input_map, preferred_element_type=jnp.float32
    )
    zero_state = jnp.zeros((head_count, head_size, state_size), jnp.float32)
    zero_log = jnp.zeros((head_count,), jnp.float32)
    running_state = zero_state
    running_log = zero_log
    position = 0
    prefix_states = running_state
    prefix_logs = running_log
    running_state = (
        jnp.exp(block_log[position])[:, None, None] * running_state + local_state[position]
    )
    running_log = block_log[position]
    device_log = running_log
    entry_device = carried_in((device_log, running_state), "seq", combine, (zero_log, zero_state))[
        1
    ]
    entry_state = jnp.stack([jnp.exp(prefix_logs)[:, None, None] * entry_device + prefix_states])
    entry_bf = entry_state.astype(jnp.bfloat16)
    outputs = jnp.einsum(
        "bhts,bshp->bthp", mixing, value_blocks, preferred_element_type=jnp.float32
    )
    outputs = outputs + leading_decay[..., None] * jnp.einsum(
        "btn,bhpn->bthp", output_map, entry_bf, preferred_element_type=jnp.float32
    )
    outputs = outputs + skip_gain[None, None, :, None] * value_blocks
    token_weight = conf_float * doc_len / conf_total
    target = teacher.reshape(blocks, GROUP, head_count, head_size)
    out_grad = (token_weight.reshape(blocks, GROUP)[:, :, None, None] * (outputs - target)).astype(
        jnp.bfloat16
    )
    out_scaled = (leading_decay[..., None] * out_grad).astype(jnp.bfloat16)
    state_pull = jnp.einsum(
        "bthp,btn->bhpn", out_scaled, output_map, preferred_element_type=jnp.float32
    )
    suffix_grads = [zero_state] * blocks
    suffix_logs = [zero_log] * blocks
    running_grad = zero_state
    running_log = zero_log
    position = 0
    suffix_grads[position] = running_grad
    suffix_logs[position] = running_log
    running_grad = jnp.exp(block_log[position])[:, None, None] * running_grad + state_pull[position]
    after_grad = prefix((device_log, running_grad), "seq", combine, (zero_log, zero_state))[1]
    exit_grad = jnp.stack([jnp.exp(suffix_logs[0])[:, None, None] * after_grad + suffix_grads[0]])
    exit_bf = exit_grad.astype(jnp.bfloat16)
    pair_dots = jnp.einsum(
        "bthp,bshp->bhts", out_grad, value_blocks, preferred_element_type=jnp.float32
    )
    score_grad = jnp.sum(pair_dots * decay_grid, axis=1).astype(jnp.bfloat16)
    values_grad = jnp.einsum(
        "bhts,bthp->bshp", mixing, out_grad, preferred_element_type=jnp.float32
    )
    values_grad = values_grad + write_scale[..., None] * jnp.einsum(
        "bsn,bhpn->bshp", input_map, exit_bf, preferred_element_type=jnp.float32
    )
    values_grad = values_grad + skip_gain[None, None, :, None] * out_grad
    input_grad = jnp.einsum(
        "bts,btn->bsn", score_grad, output_map, preferred_element_type=jnp.float32
    )
    input_grad = input_grad + jnp.einsum(
        "bshp,bhpn->bsn", value_scaled, exit_bf, preferred_element_type=jnp.float32
    )
    output_grad = jnp.einsum(
        "bts,bsn->btn", score_grad, input_map, preferred_element_type=jnp.float32
    )
    output_grad = output_grad + jnp.einsum(
        "bthp,bhpn->btn", out_scaled, entry_bf, preferred_element_type=jnp.float32
    )
    bc_grad = (
        jnp.concatenate([input_grad, output_grad], axis=2)
        .reshape(length, 2 * state_size)
        .astype(jnp.bfloat16)
    )
    contract_cols = (((1,), (1,)), ((), ()))
    hidden_acc = lax.dot_general(
        bc_grad, full_weight, contract_cols, preferred_element_type=jnp.float32
    )
    hidden_grad = hidden_acc.astype(jnp.bfloat16)
    contract_rows = (((0,), (0,)), ((), ()))
    local_rows = bc_weight.shape[0]
    full_term = lax.dot_general(
        hidden_in, bc_grad, contract_rows, preferred_element_type=jnp.float32
    )
    summed = lax.psum(full_term, ("dp", "seq"))
    own_rows = lax.dynamic_slice_in_dim(summed, lax.axis_index("dp") * local_rows, local_rows, 0)
    weight_grad = own_rows / math.sqrt(all_tokens)
    return (
        values_grad.reshape(length, head_count * head_size).astype(jnp.bfloat16),
        hidden_grad,
        weight_grad,
    )


def solution(mesh):
    return jax.shard_map(
        body,
        mesh=mesh,
        in_specs=(
            P(("dp", "seq"), None),
            P("dp", None),
            P(("dp", "seq"), None),
            P(("dp", "seq"), None),
            P(("dp", "seq"), None),
            P(("dp", "seq")),
            P(),
            P(),
            P(("dp", "seq")),
        ),
        out_specs=(P(("dp", "seq"), None), P(("dp", "seq"), None), P("dp", None)),
        check_vma=False,
    )
```

profile of v0, /device:TPU:2, one launch (start us, length us, event | category | flops | bytes accessed | tf_op | source)
XLA Modules:
  0.0 555.4 jit_solution(11231758227764263669)
XLA Ops:
  11.6 4.1 copy.66
  15.7 3.3 fusion.11
  19.0 71.0 %all-gather.8.cloned.1.call-done = bf16[4096,256]{1,0:T(8,128)(2,1)} async-done(((bf16[64,256]{1,0:T(8,128)(2,1)}), bf16[4096,256]{1,0:T(8,128)(2,1)}) %all-gather.8.cloned.1.call-update) | async-done | bytes 2097168 | tf_op jit(solution)/shard_map/all_gather | solution.py:82
  95.9 11.1 %psum.14 = f32[]{:T(128)} all-reduce(f32[]{:T(128)} %convert_reduce_fusion), channel_id=1, replica_groups=mesh['dp'=64,'seq'=4] {'seq'}, use_global_device_ids=true, to_apply=%region_1.0 | all-reduce | flops 1 | bytes 8 | tf_op jit(solution)/shard_map/psum | solution.py:81
  107.3 4.4 copy.72
  111.8 6.9 %all-gather = f32[4,1,64]{2,1,0:T(1,128)S(1)} all-gather(f32[1,1,64]{2,1,0:T(1,128)S(1)} %get-tuple-element.317), channel_id=2, replica_groups=mesh['dp'=64,'seq'=4] {'seq'}, dimensions={0}, use_global_device_ids=true | all-gather | bytes 1280 | tf_op jit(solution)/shard_map/all_gather | solution.py:14
  119.6 59.5 %all-gather.10.cloned.1.call-done = f32[256,64,128]{2,1,0:T(8,128)} async-done(((f32[64,64,128]{2,1,0:T(8,128)}), f32[256,64,128]{2,1,0:T(8,128)}) %all-gather.10.cloned.1.call-update) | async-done | bytes 8388624 | tf_op jit(solution)/shard_map/all_gather | solution.py:14
  179.1 14.9 %while.30 = (s32[]{:T(128)}, f32[64,64,128]{2,1,0:T(8,128)}, s32[]{:T(128)}, f32[4,64]{1,0:T(4,128)S(1)}, f32[4,64,64,128]{3,2,1,0:T(8,128)}, /*index=5*/s32[]{:T(128)}, s32[]{:T(128)}) while((s32[]{:T(128)}, f32[64,64,128]{2,1,0:T(8,128)}, s32[]{:T(128)}, f32[4,64]{1,0:T(4,128)S(1)}, f32[4,64,64,128]{3,2,1,0:T(8,128)}, ...), condition=%wide.region_5.6_spmd.clone, body=%wide.region_4.5_spmd.clone.sunk | while | flops 2097156 | bytes 6292329 | solution.py:24
  179.1 3.2 fusion.71
  182.4 3.9 fusion.71
  186.3 3.9 fusion.71
  190.2 3.9 fusion.71
  197.5 6.2 %fusion.10 = bf16[1,256,64,64]{1,3,2,0:T(8,128)(2,1)S(1)} fusion(f32[1,256,64,64]{1,3,2,0:T(8,128)S(1)} %bitcast.161, f32[256,64,64]{0,2,1:T(8,128)S(1)} %fusion.33, bf16[256,64,64]{0,2,1:T(8,128)(2,1)S(1)} %bitcast.157, f32[64,256]{1,0:T(8,128)S(1)} %copy.65, f32[64,256]{1,0:T(8,128)S(1)} %bitcast_add_fusion.4, f32[256,256]{1,0:T(8,128)S(1)} %fusion.41, ...), kind=kOutput, calls=%fused_computation.23 | convolution fusion | flops 570425344 | bytes 15205632 | tf_op jit(solution)/shard_map/bhts,bshp->bthp/dot_general | solution.py:129
  206.8 8.8 %all-gather.3 = bf16[4,1,64]{2,1,0:T(2,128)(2,1)S(1)} all-gather(bf16[1,1,64]{2,1,0:T(2,128)(2,1)S(1)} %slice.61), channel_id=5, replica_groups=mesh['dp'=64,'seq'=4] {'seq'}, dimensions={0}, use_global_device_ids=true | all-gather | bytes 640 | tf_op jit(solution)/shard_map/all_gather | solution.py:30
  219.1 6.9 %multiply_reduce_fusion = bf16[256,256]{1,0:T(8,128)(2,1)S(1)} fusion(bf16[256,64,64]{0,2,1:T(8,128)(2,1)S(1)} %bitcast.159, f32[64,256]{1,0:T(8,128)S(1)} %copy.65, f32[64,256]{1,0:T(8,128)S(1)} %bitcast_add_fusion.4, pred[256,256]{1,0:T(8,128)(4,1)S(1)} %iota_compare_fusion, bf16[1,256,64,64]{1,3,2,0:T(8,128)(2,1)S(1)} %copy-done.6), kind=kOutput, calls=%fused_computation.6 | convolution fusion | flops 561971200 | bytes 4521984 | tf_op jit(solution)/shard_map/bthp,bshp->bhts/dot_general | solution.py:156
  226.3 32.4 %all-gather.12.cloned.1.call-done = bf16[256,64,128]{2,1,0:T(8,128)(2,1)} async-done(((bf16[64,64,128]{2,1,0:T(8,128)(2,1)}), bf16[256,64,128]{2,1,0:T(8,128)(2,1)}) %all-gather.12.cloned.1.call-update) | async-done | bytes 4194320 | tf_op jit(solution)/shard_map/all_gather | solution.py:30
  258.7 13.7 %while.31 = (s32[]{:T(128)}, f32[64,64,128]{2,1,0:T(8,128)}, s32[]{:T(128)}, bf16[4,64]{1,0:T(4,128)(2,1)S(1)}, bf16[4,64,64,128]{3,2,1,0:T(8,128)(2,1)}, /*index=5*/s32[]{:T(128)}, s32[]{:T(128)}, s32[]{:T(128)}, s32[]{:T(128)}) while((s32[]{:T(128)}, f32[64,64,128]{2,1,0:T(8,128)}, s32[]{:T(128)}, bf16[4,64]{1,0:T(4,128)(2,1)S(1)}, ...), condition=%wide.region_7.8_spmd.clone, body=%wide.region_6.7_spmd.clone.sunk | while | flops 2621512 | bytes 5243687 | solution.py:44
  261.7 3.6 fusion.72
  265.2 3.6 fusion.72
  268.8 3.6 fusion.72
  280.6 6.8 %fusion.6 = bf16[1,256,64,64]{1,3,2,0:T(8,128)(2,1)} fusion(bf16[1,256,64,64]{1,3,2,0:T(8,128)(2,1)S(1)} %copy-done.7, f32[256,64,64]{0,2,1:T(8,128)S(1)} %fusion.30, f32[64,256]{1,0:T(8,128)S(1)} %copy.65, f32[64,256]{1,0:T(8,128)S(1)} %bitcast_add_fusion.4, f32[256,256]{1,0:T(8,128)S(1)} %fusion.41, pred[256,256]{1,0:T(8,128)(4,1)S(1)} %iota_compare_fusion, ...), kind=kOutput, calls=%fused_computation.17 | convolution fusion | flops 568328192 | bytes 8913152 | tf_op jit(solution)/shard_map/bhts,bthp->bshp/dot_general | solution.py:160
  287.4 4.1 copy.74
  291.5 3.7 convolution_convert_fusion
  295.2 252.0 %all-reduce.2.cloned.1.call-done = f32[4096,256]{0,1:T(8,128)} async-done(((f32[4096,256]{0,1:T(8,128)}), f32[4096,256]{0,1:T(8,128)}) %all-reduce.2.cloned.1.call-update) | async-done | bytes 4194320 | tf_op jit(solution)/shard_map/psum | solution.py:194
  (78 shorter events, 34.4 us)
Async XLA Ops:
  7.2 82.9 %copy-start = (bf16[256,4096]{1,0:T(8,128)(2,1)S(1)}, bf16[256,4096]{1,0:T(8,128)(2,1)}, u32[]{:S(2)}) copy-start(bf16[256,4096]{1,0:T(8,128)(2,1)} %param.13) | copy-start | bytes 6291460
  7.2 82.9 %all-gather.8.cloned.1.call-start = ((), (), s32[]{:S(2)}) async-start(), calls=%async_computation | async-start | bytes 2129920 | tf_op jit(solution)/shard_map/all_gather | solution.py:82
  7.9 171.2 %all-gather.10.cloned.1.call-start = ((), (), s32[]{:S(2)}) async-start(), calls=%async_computation.2 | async-start | bytes 10485760 | tf_op jit(solution)/shard_map/all_gather | solution.py:14
  90.1 2.5 copy-start.1
  94.6 0.7 copy-start.8
  94.6 164.1 %all-gather.12.cloned.1.call-start = ((), (), s32[]{:S(2)}) async-start(), calls=%async_computation.3 | async-start | bytes 5242880 | tf_op jit(solution)/shard_map/all_gather | solution.py:30
  194.0 2.5 copy-start.2
  194.0 3.5 copy-start.4
  194.0 3.5 copy-start.9
  203.7 1.4 copy-start.5
  206.7 340.5 %all-reduce.2.cloned.1.call-start = ((), (), s32[]{:S(2)}) async-start(), calls=%async_computation.1 | async-start | bytes 8388608 | tf_op jit(solution)/shard_map/psum | solution.py:194
  215.6 3.0 copy-start.3
  215.6 3.5 copy-start.6
  278.1 2.5 copy-start.7
Sparse Core Ops, SparseCore 0:
  10.8 79.2 all-gather.7
  94.7 84.3 all-gather.9
  206.9 51.7 all-gather.11
  278.2 268.8 all-reduce.1
where the time goes:
time: 556 us; the launch traced here: 555 us
  waiting for transfers between devices  416 us (75%)
  matrix products  43.8 us (8%)
  other arithmetic  36.4 us (7%)
  blocking collectives  26.8 us (5%)
  local copies, waits for them, and re-layouts  18.5 us (3%)
  between operations  14 us (3%)
    psum x1, waiting for transfers between devices, body(): summed = lax.psum(full_term, ('dp', 'seq'))  252 us
    all_gather x1, waiting for transfers between devices, body(): full_weight = lax.all_gather(bc_weight, 'dp', axis=0, tiled=True)  71 us
    all_gather x1, waiting for transfers between devices, carried_in(): everything = jax.tree.map(lambda part: lax.all_gather(part, axis), x)  59.5 us
    all_gather x1, waiting for transfers between devices, prefix(): lax.all_gather(part.astype(kind), axis)  32.4 us
    select_n x4, other arithmetic, carried_step(): return jax.tree.map(lambda a, b: jnp.where(reached, a, b), new, before)  14.9 us
    select_n x4, other arithmetic, prefix_step(): return jax.tree.map(lambda a, b: jnp.where(reached, a, b), new, before)  13.7 us
    unnamed x25, local copies, waits for them, and re-layouts  13.3 us
    psum x1, blocking collectives, body(): conf_total = lax.psum(jnp.sum(conf_float), 'seq')  11.1 us
  transfers between devices with their start and end apart: 4, of which 4 were waited for; matrix products, arithmetic and copies ran while one was open for 8% of the time, Pallas kernels for 0%

commit v1 on v0

--- a/solution.py
+++ b/solution.py
@@ -191,7 +191,7 @@
     full_term = lax.dot_general(
         hidden_in, bc_grad, contract_rows, preferred_element_type=jnp.float32
     )
-    summed = lax.psum(full_term, ("dp", "seq"))
+    summed = lax.psum(lax.psum(full_term, "seq"), "dp")
     own_rows = lax.dynamic_slice_in_dim(summed, lax.axis_index("dp") * local_rows, local_rows, 0)
     weight_grad = own_rows / math.sqrt(all_tokens)
     return (

time: 556 us -> 585 us (1.052)
  waiting for transfers between devices: 416 us -> 444 us
    psum x1 -> x2, waiting for transfers between devices: 252 us -> 280 us  [body(): summed = lax.psum(lax.psum(full_term, 'seq'), 'dp')]
  transfers between devices with their start and end apart: 4 -> 5, of which waited for: 4 -> 5; matrix products, arithmetic and copies ran while one was open for 8% -> 8% of each run, Pallas kernels for 0% -> 0%
where the time goes in v1:
time: 585 us; the launch traced here: 584 us
  waiting for transfers between devices  444 us (76%)
  matrix products  44 us (8%)
  other arithmetic  36.4 us (6%)
  blocking collectives  26.7 us (5%)
  local copies, waits for them, and re-layouts  18.5 us (3%)
  between operations  14.1 us (2%)
    psum x2, waiting for transfers between devices, body(): summed = lax.psum(lax.psum(full_term, 'seq'), 'dp')  280 us
    all_gather x1, waiting for transfers between devices, body(): full_weight = lax.all_gather(bc_weight, 'dp', axis=0, tiled=True)  71 us
    all_gather x1, waiting for transfers between devices, carried_in(): everything = jax.tree.map(lambda part: lax.all_gather(part, axis), x)  59.5 us
    all_gather x1, waiting for transfers between devices, prefix(): lax.all_gather(part.astype(kind), axis)  32.6 us
    select_n x4, other arithmetic, carried_step(): return jax.tree.map(lambda a, b: jnp.where(reached, a, b), new, before)  14.9 us
    select_n x4, other arithmetic, prefix_step(): return jax.tree.map(lambda a, b: jnp.where(reached, a, b), new, before)  13.7 us
    unnamed x25, local copies, waits for them, and re-layouts  13.2 us
  transfers between devices with their start and end apart: 5, of which 5 were waited for; matrix products, arithmetic and copies ran while one was open for 8% of the time, Pallas kernels for 0%

profile of v1, /device:TPU:2, one launch (start us, length us, event | category | flops | bytes accessed | tf_op | source)
XLA Modules:
  0.0 584.1 jit_solution(787419911868357663)
XLA Ops:
  11.6 4.1 copy.66
  15.7 3.3 fusion.11
  19.0 71.0 %all-gather.8.cloned.1.call-done = bf16[4096,256]{1,0:T(8,128)(2,1)} async-done(((bf16[64,256]{1,0:T(8,128)(2,1)}), bf16[4096,256]{1,0:T(8,128)(2,1)}) %all-gather.8.cloned.1.call-update) | async-done | bytes 2097168 | tf_op jit(solution)/shard_map/all_gather | solution.py:82
  95.9 11.1 %psum.21 = f32[]{:T(128)} all-reduce(f32[]{:T(128)} %convert_reduce_fusion), channel_id=1, replica_groups=mesh['dp'=64,'seq'=4] {'seq'}, use_global_device_ids=true, to_apply=%region_1.0 | all-reduce | flops 1 | bytes 8 | tf_op jit(solution)/shard_map/psum | solution.py:81
  107.3 4.4 copy.72
  111.8 6.9 %all-gather = f32[4,1,64]{2,1,0:T(1,128)S(1)} all-gather(f32[1,1,64]{2,1,0:T(1,128)S(1)} %get-tuple-element.317), channel_id=2, replica_groups=mesh['dp'=64,'seq'=4] {'seq'}, dimensions={0}, use_global_device_ids=true | all-gather | bytes 1280 | tf_op jit(solution)/shard_map/all_gather | solution.py:14
  119.6 59.5 %all-gather.10.cloned.1.call-done = f32[256,64,128]{2,1,0:T(8,128)} async-done(((f32[64,64,128]{2,1,0:T(8,128)}), f32[256,64,128]{2,1,0:T(8,128)}) %all-gather.10.cloned.1.call-update) | async-done | bytes 8388624 | tf_op jit(solution)/shard_map/all_gather | solution.py:14
  179.1 14.9 %while.30 = (s32[]{:T(128)}, f32[64,64,128]{2,1,0:T(8,128)}, s32[]{:T(128)}, f32[4,64]{1,0:T(4,128)S(1)}, f32[4,64,64,128]{3,2,1,0:T(8,128)}, /*index=5*/s32[]{:T(128)}, s32[]{:T(128)}) while((s32[]{:T(128)}, f32[64,64,128]{2,1,0:T(8,128)}, s32[]{:T(128)}, f32[4,64]{1,0:T(4,128)S(1)}, f32[4,64,64,128]{3,2,1,0:T(8,128)}, ...), condition=%wide.region_5.6_spmd.clone, body=%wide.region_4.5_spmd.clone.sunk | while | flops 2097156 | bytes 6292329 | solution.py:24
  182.4 3.9 fusion.71
  186.3 3.9 fusion.71
  190.2 3.9 fusion.71
  197.5 6.2 %fusion.10 = bf16[1,256,64,64]{1,3,2,0:T(8,128)(2,1)S(1)} fusion(f32[1,256,64,64]{1,3,2,0:T(8,128)S(1)} %bitcast.161, f32[256,64,64]{0,2,1:T(8,128)S(1)} %fusion.33, bf16[256,64,64]{0,2,1:T(8,128)(2,1)S(1)} %bitcast.157, f32[64,256]{1,0:T(8,128)S(1)} %copy.65, f32[64,256]{1,0:T(8,128)S(1)} %bitcast_add_fusion.4, f32[256,256]{1,0:T(8,128)S(1)} %fusion.41, ...), kind=kOutput, calls=%fused_computation.23 | convolution fusion | flops 570425344 | bytes 15205632 | tf_op jit(solution)/shard_map/bhts,bshp->bthp/dot_general | solution.py:129
  206.8 8.6 %all-gather.3 = bf16[4,1,64]{2,1,0:T(2,128)(2,1)S(1)} all-gather(bf16[1,1,64]{2,1,0:T(2,128)(2,1)S(1)} %slice.61), channel_id=5, replica_groups=mesh['dp'=64,'seq'=4] {'seq'}, dimensions={0}, use_global_device_ids=true | all-gather | bytes 640 | tf_op jit(solution)/shard_map/all_gather | solution.py:30
  218.9 6.9 %multiply_reduce_fusion = bf16[256,256]{1,0:T(8,128)(2,1)S(1)} fusion(bf16[256,64,64]{0,2,1:T(8,128)(2,1)S(1)} %bitcast.159, f32[64,256]{1,0:T(8,128)S(1)} %copy.65, f32[64,256]{1,0:T(8,128)S(1)} %bitcast_add_fusion.4, pred[256,256]{1,0:T(8,128)(4,1)S(1)} %iota_compare_fusion, bf16[1,256,64,64]{1,3,2,0:T(8,128)(2,1)S(1)} %copy-done.6), kind=kOutput, calls=%fused_computation.6 | convolution fusion | flops 561971200 | bytes 4521984 | tf_op jit(solution)/shard_map/bthp,bshp->bhts/dot_general | solution.py:156
  226.0 32.6 %all-gather.12.cloned.1.call-done = bf16[256,64,128]{2,1,0:T(8,128)(2,1)} async-done(((bf16[64,64,128]{2,1,0:T(8,128)(2,1)}), bf16[256,64,128]{2,1,0:T(8,128)(2,1)}) %all-gather.12.cloned.1.call-update) | async-done | bytes 4194320 | tf_op jit(solution)/shard_map/all_gather | solution.py:30
  258.7 13.7 %while.31 = (s32[]{:T(128)}, f32[64,64,128]{2,1,0:T(8,128)}, s32[]{:T(128)}, bf16[4,64]{1,0:T(4,128)(2,1)S(1)}, bf16[4,64,64,128]{3,2,1,0:T(8,128)(2,1)}, /*index=5*/s32[]{:T(128)}, s32[]{:T(128)}, s32[]{:T(128)}, s32[]{:T(128)}) while((s32[]{:T(128)}, f32[64,64,128]{2,1,0:T(8,128)}, s32[]{:T(128)}, bf16[4,64]{1,0:T(4,128)(2,1)S(1)}, ...), condition=%wide.region_7.8_spmd.clone, body=%wide.region_6.7_spmd.clone.sunk | while | flops 2621512 | bytes 5243687 | solution.py:44
  261.7 3.6 fusion.72
  265.2 3.6 fusion.72
  268.8 3.6 fusion.72
  278.4 98.2 %all-reduce.3.cloned.1.call-done = f32[4096,256]{0,1:T(8,128)} async-done(((f32[4096,256]{0,1:T(8,128)}), f32[4096,256]{0,1:T(8,128)}) %all-reduce.3.cloned.1.call-update) | async-done | bytes 4194320 | tf_op jit(solution)/shard_map/psum | solution.py:194
  379.1 6.8 %fusion.6 = bf16[1,256,64,64]{1,3,2,0:T(8,128)(2,1)} fusion(bf16[1,256,64,64]{1,3,2,0:T(8,128)(2,1)S(1)} %copy-done.7, f32[256,64,64]{0,2,1:T(8,128)S(1)} %fusion.30, f32[64,256]{1,0:T(8,128)S(1)} %copy.65, f32[64,256]{1,0:T(8,128)S(1)} %bitcast_add_fusion.4, f32[256,256]{1,0:T(8,128)S(1)} %fusion.41, pred[256,256]{1,0:T(8,128)(4,1)S(1)} %iota_compare_fusion, ...), kind=kOutput, calls=%fused_computation.17 | convolution fusion | flops 568328192 | bytes 8913152 | tf_op jit(solution)/shard_map/bhts,bthp->bshp/dot_general | solution.py:160
  385.9 4.1 copy.74
  390.0 3.9 convolution_convert_fusion
  393.9 181.9 %all-reduce.5.cloned.1.call-done = f32[4096,256]{0,1:T(8,128)} async-done(((f32[4096,256]{0,1:T(8,128)}), f32[4096,256]{0,1:T(8,128)}) %all-reduce.5.cloned.1.call-update) | async-done | bytes 4194320 | tf_op jit(solution)/shard_map/psum | solution.py:194
  (81 shorter events, 37.9 us)
Async XLA Ops:
  7.2 82.9 %copy-start = (bf16[256,4096]{1,0:T(8,128)(2,1)S(1)}, bf16[256,4096]{1,0:T(8,128)(2,1)}, u32[]{:S(2)}) copy-start(bf16[256,4096]{1,0:T(8,128)(2,1)} %param.13) | copy-start | bytes 6291460
  7.2 82.9 %all-gather.8.cloned.1.call-start = ((), (), s32[]{:S(2)}) async-start(), calls=%async_computation | async-start | bytes 2129920 | tf_op jit(solution)/shard_map/all_gather | solution.py:82
  7.9 171.2 %all-gather.10.cloned.1.call-start = ((), (), s32[]{:S(2)}) async-start(), calls=%async_computation.3 | async-start | bytes 10485760 | tf_op jit(solution)/shard_map/all_gather | solution.py:14
  90.1 2.5 copy-start.1
  94.6 0.7 copy-start.8
  94.6 164.1 %all-gather.12.cloned.1.call-start = ((), (), s32[]{:S(2)}) async-start(), calls=%async_computation.4 | async-start | bytes 5242880 | tf_op jit(solution)/shard_map/all_gather | solution.py:30
  194.0 2.5 copy-start.2
  194.0 3.5 copy-start.4
  194.0 3.5 copy-start.9
  203.7 1.4 copy-start.5
  206.7 169.9 %all-reduce.3.cloned.1.call-start = ((), (), s32[]{:S(2)}) async-start(), calls=%async_computation.1 | async-start | bytes 8388608 | tf_op jit(solution)/shard_map/psum | solution.py:194
  215.4 3.0 copy-start.3
  215.4 3.5 copy-start.6
  278.1 297.7 %all-reduce.5.cloned.1.call-start = ((), (), s32[]{:S(2)}) async-start(), calls=%async_computation.2 | async-start | bytes 8388608 | tf_op jit(solution)/shard_map/psum | solution.py:194
  376.6 2.5 copy-start.7
Sparse Core Ops, SparseCore 0:
  10.8 79.2 all-gather.7
  94.7 84.3 all-gather.9
  206.9 51.7 all-gather.11
  278.2 98.2 all-reduce.2
  380.4 195.3 all-reduce.4
